TPU v7x, 256 devices: a whole 4x4x8 slice. The times are simulated.
256 devices in a mesh: seq: 64 (over x, z, core), head: 4 (over y).
Axes of the slice: x: 4, y: 4, z: 8, core: 2. Of those that a mesh axis runs over, the one named last changes fastest.
Arguments:
- queries: bfloat16 [65536, 2048], P('seq', 'head'), may hold values from -1.796875 to 1.796875
- keys: bfloat16 [65536, 2048], P('seq', 'head'), may hold values from -1.796875 to 1.796875
- values: bfloat16 [65536, 2048], P('seq', 'head'), may hold values from -16 to 16
- grad_out: bfloat16 [65536, 2048], P('seq', 'head'), may hold values from -1.1953125 to 1.1953125
Outputs:
- output: bfloat16 [65536, 2048], P('seq', 'head')
- grad_query: bfloat16 [65536, 2048], P('seq', 'head')
- grad_key: bfloat16 [65536, 2048], P('seq', 'head')
- grad_value: bfloat16 [65536, 2048], P('seq', 'head')
All inputs are finite; a program needn't handle non-finite values.
Results may differ from a plain program's by a relative error of at most 0.0065.
Values sent between devices are 32-bit elements; how exact they have to be, the bound alone decides.
A program may use at most 128 MiB of HBM per device.

v0:
```python
import jax
import jax.numpy as jnp
from jax import lax
from jax.sharding import PartitionSpec as P

HEADS = 16
HEAD_DIM = 128
EPSILON = 1e-06


def entering(shard, axis, combine, identity, reverse):
    size, here = (lax.axis_size(axis), lax.axis_index(axis))
    everything = lax.all_gather(shard, axis)
    start = jnp.broadcast_to(jnp.asarray(identity, shard.dtype), shard.shape)

    def step(k, before):
        at = size - 1 - k if reverse else k
        reached = at > here if reverse else at < here
        new = combine(before, everything[at])
        return jnp.where(reached, new, before)

    return lax.fori_loop(0, size, step, start)


def add_states(earlier, later):
    return earlier + later


def masked_scores(query_side, key_side):
    raw_scores = jnp.einsum(
        "thd,shd->hts", query_side, key_side, preferred_element_type=jnp.float32
    )
    count = query_side.shape[0]
    row_index = lax.broadcasted_iota(jnp.int32, (count, count), 0)
    col_index = lax.broadcasted_iota(jnp.int32, (count, count), 1)
    keep = (row_index >= col_index)[None]
    return jnp.where(keep, raw_scores, jnp.zeros_like(raw_scores)).astype(jnp.bfloat16)


def shards(queries, keys, values, grad_out):
    tok_rows = queries.shape[0]
    local_heads = queries.shape[1] // HEAD_DIM
    shaped = (tok_rows, local_heads, HEAD_DIM)
    full_width = HEADS * HEAD_DIM
    query_rows = queries.reshape(shaped)
    key_rows = keys.reshape(shaped)
    value_rows = values.reshape(shaped)
    local_state = jnp.einsum(
        "thd,the->hde", key_rows, value_rows, preferred_element_type=jnp.float32
    )
    zero_state = jnp.zeros_like(local_state)
    prefix = entering(local_state, "seq", add_states, zero_state, False)
    scores = masked_scores(query_rows, key_rows)
    prefix_round = prefix.astype(jnp.bfloat16)
    mixed = jnp.einsum("hts,she->the", scores, value_rows, preferred_element_type=jnp.float32)
    mixed = mixed + jnp.einsum(
        "thd,hde->the", query_rows, prefix_round, preferred_element_type=jnp.float32
    )
    mixed_rows = mixed.reshape(tok_rows, -1)
    grad_float = grad_out.astype(jnp.float32)
    squares = lax.psum(jnp.sum(mixed_rows * mixed_rows, axis=1), "head")
    inverse_rms = lax.rsqrt(squares / full_width + EPSILON)
    normed = mixed_rows * inverse_rms[:, None]
    crossed = lax.psum(jnp.sum(grad_float * normed, axis=1), "head")
    cross_mean = (crossed / full_width)[:, None]
    output = normed.astype(jnp.bfloat16)
    grad_mixed = (
        (inverse_rms[:, None] * (grad_float - normed * cross_mean))
        .astype(jnp.bfloat16)
        .reshape(shaped)
    )
    grad_state = jnp.einsum(
        "thd,the->hde", query_rows, grad_mixed, preferred_element_type=jnp.float32
    )
    suffix = entering(grad_state, "seq", add_states, zero_state, True)
    suffix_round = suffix.astype(jnp.bfloat16)
    grad_scores = masked_scores(grad_mixed, value_rows)
    grad_q = jnp.einsum("hts,shd->thd", grad_scores, key_rows, preferred_element_type=jnp.float32)
    grad_q = grad_q + jnp.einsum(
        "the,hde->thd", grad_mixed, prefix_round, preferred_element_type=jnp.float32
    )
    grad_k = jnp.einsum("hts,thd->shd", grad_scores, query_rows, preferred_element_type=jnp.float32)
    grad_k = grad_k + jnp.einsum(
        "she,hde->shd", value_rows, suffix_round, preferred_element_type=jnp.float32
    )
    grad_v = jnp.einsum("hts,the->she", scores, grad_mixed, preferred_element_type=jnp.float32)
    grad_v = grad_v + jnp.einsum(
        "shd,hde->she", key_rows, suffix_round, preferred_element_type=jnp.float32
    )
    flat_shape = (tok_rows, local_heads * HEAD_DIM)
    return (
        output,
        grad_q.astype(jnp.bfloat16).reshape(flat_shape),
        grad_k.astype(jnp.bfloat16).reshape(flat_shape),
        grad_v.astype(jnp.bfloat16).reshape(flat_shape),
    )


def solution(mesh):
    return jax.shard_map(
        shards,
        mesh=mesh,
        in_specs=(P("seq", "head"), P("seq", "head"), P("seq", "head"), P("seq", "head")),
        out_specs=(P("seq", "head"), P("seq", "head"), P("seq", "head"), P("seq", "head")),
        check_vma=False,
    )
```

profile of v0, /device:TPU:1, one launch (start us, length us, event | category | flops | bytes accessed | tf_op | source)
XLA Modules:
  0.0 399.9 jit_solution(9009849528236782950)
XLA Ops:
  7.2 2.4 copy.100
  9.6 2.4 fusion.10
  13.5 2.5 select_convert_fusion.1
  16.0 3.2 copy-done.1
  19.3 2.9 fusion.5
  22.2 94.0 %all-gather.5.cloned.1.call-done = f32[256,128,128]{2,1,0:T(8,128)} async-done(((f32[4,128,128]{2,1,0:T(8,128)}), f32[256,128,128]{2,1,0:T(8,128)}) %all-gather.5.cloned.1.call-update) | async-done | bytes 16777232 | tf_op jit(solution)/shard_map/all_gather | solution.py:13
  116.2 68.1 %while.30 = (s32[]{:T(128)}, f32[4,128,128]{2,1,0:T(8,128)S(1)}, s32[]{:T(128)}, f32[64,4,128,128]{3,2,1,0:T(8,128)}, s32[]{:T(128)}, /*index=5*/s32[]{:T(128)}) while((s32[]{:T(128)}, f32[4,128,128]{2,1,0:T(8,128)S(1)}, s32[]{:T(128)}, f32[64,4,128,128]{3,2,1,0:T(8,128)}, s32[]{:T(128)}, /*index=5*/s32[]{:T(128)}) %tuple.87), condition=%wide.region_1.2_spmd.clone, body=%wide.region_0.1_spmd.clone.sunk | while | flops 196612 | bytes 786533 | solution.py:22
  184.3 1.8 multiply_reduce_fusion
  186.1 8.4 %psum.14 = f32[1024]{0:T(1024)S(1)} all-reduce(f32[1024]{0:T(1024)S(1)} %get-tuple-element.255), channel_id=1, replica_groups=mesh['seq'=64,'head'=4] {'head'}, use_global_device_ids=true, to_apply=%region_3.4 | all-reduce | flops 1024 | bytes 8192 | tf_op jit(solution)/shard_map/psum | solution.py:61
  194.5 1.9 copy.38
  196.5 1.7 fusion
  198.2 6.0 %psum.15 = f32[1024]{0:T(1024)S(1)} all-reduce(f32[1024]{0:T(1024)S(1)} %fusion), channel_id=1, replica_groups=mesh['seq'=64,'head'=4] {'head'}, use_global_device_ids=true, to_apply=%region_5.6 | all-reduce | flops 1024 | bytes 8192 | tf_op jit(solution)/shard_map/psum | solution.py:64
  204.2 3.0 fusion.2
  207.2 1.5 copy.56
  210.0 4.3 %select_convert_fusion = bf16[4,1024,1024]{2,1,0:T(8,128)(2,1)S(1)} fusion(bf16[1024,4,128]{0,2,1:T(8,128)(2,1)S(1)} %bitcast.105, pred[1024,1024]{1,0:T(8,128)(4,1)} %copy-done.10, bf16[1024,512]{1,0:T(8,128)(2,1)} %param.10), kind=kOutput, calls=%fused_computation.2 | convolution fusion | flops 1082130432 | bytes 11534336 | tf_op jit(solution)/shard_map/thd,shd->hts/dot_general | solution.py:30
  214.4 2.9 fusion.32
  219.0 2.3 copy.51
  221.3 6.2 %fusion.33 = f32[4,128,1024]{2,1,0:T(8,128)} fusion(bf16[1024,4,128]{0,2,1:T(8,128)(2,1)S(1)} %bitcast.107, bf16[4,1024,1024]{2,1,0:T(8,128)(2,1)} %copy-done.1), kind=kOutput, calls=%fused_computation.49 | convolution fusion | flops 1073741824 | bytes 11534336 | tf_op jit(solution)/shard_map/hts,the->she/dot_general | solution.py:86
  227.5 82.1 %all-gather.7.cloned.1.call-done = f32[256,128,128]{2,1,0:T(8,128)} async-done(((f32[4,128,128]{2,1,0:T(8,128)}), f32[256,128,128]{2,1,0:T(8,128)}) %all-gather.7.cloned.1.call-update) | async-done | bytes 16777232 | tf_op jit(solution)/shard_map/all_gather | solution.py:13
  309.6 68.4 %while.31 = (s32[]{:T(128)}, f32[4,128,128]{2,1,0:T(8,128)S(1)}, s32[]{:T(128)}, f32[64,4,128,128]{3,2,1,0:T(8,128)}, s32[]{:T(128)}, /*index=5*/s32[]{:T(128)}, s32[]{:T(128)}, s32[]{:T(128)}) while((s32[]{:T(128)}, f32[4,128,128]{2,1,0:T(8,128)S(1)}, s32[]{:T(128)}, f32[64,4,128,128]{3,2,1,0:T(8,128)}, s32[]{:T(128)}, ...), condition=%wide.region_7.8_spmd.clone, body=%wide.region_6.7_spmd.clone.sunk | while | flops 196616 | bytes 786595 | solution.py:22
  378.0 3.2 fusion.7
  382.7 2.4 copy.53
  385.1 5.7 %fusion.3 = bf16[1024,4,128]{0,2,1:T(8,128)(2,1)} fusion(f32[4,128,1024]{2,1,0:T(8,128)S(1)} %copy-done.4, bf16[4,1024,1024]{2,1,0:T(8,128)(2,1)} %copy-done.2, bf16[1024,512]{1,0:T(8,128)(2,1)S(1)} %copy-done), kind=kOutput, calls=%fused_computation.11 | convolution fusion | flops 1074790400 | bytes 12582912 | tf_op jit(solution)/shard_map/hts,thd->shd/dot_general | solution.py:82
  390.8 2.3 copy.52
  (162 shorter events, 139.1 us)
Async XLA Ops:
  7.2 6.3 %copy-start = (bf16[1024,512]{1,0:T(8,128)(2,1)S(1)}, bf16[1024,512]{1,0:T(8,128)(2,1)}, u32[]{:S(2)}) copy-start(bf16[1024,512]{1,0:T(8,128)(2,1)} %param.8) | copy-start | bytes 3145732
  7.2 2.5 copy-start.7
  7.2 109.0 %all-gather.5.cloned.1.call-start = ((), (), s32[]{:S(2)}) async-start(), calls=%async_computation | async-start | bytes 17039360 | tf_op jit(solution)/shard_map/all_gather | solution.py:13
  9.6 3.8 copy-start.5
  12.1 297.5 %all-gather.7.cloned.1.call-start = ((), (), s32[]{:S(2)}) async-start(), calls=%async_computation.1 | async-start | bytes 17039360 | tf_op jit(solution)/shard_map/all_gather | solution.py:13
  12.5 1.0 copy-start.10
  13.5 5.8 %copy-start.8 = (bf16[1024,512]{1,0:T(8,128)(2,1)S(1)}, bf16[1024,512]{1,0:T(8,128)(2,1)}, u32[]{:S(2)}) copy-start(bf16[1024,512]{1,0:T(8,128)(2,1)} %param.10) | copy-start | bytes 3145732
  16.0 3.2 copy-start.1
  210.0 4.4 %copy-start.9 = (bf16[1024,512]{0,1:T(8,128)(2,1)S(1)}, bf16[1024,512]{0,1:T(8,128)(2,1)}, u32[]{:S(2)}) copy-start(bf16[1024,512]{0,1:T(8,128)(2,1)} %copy.100) | copy-start | bytes 3145732
  214.4 3.2 copy-start.2
  378.0 3.2 copy-start.3
  378.0 3.2 copy-start.6
  382.7 2.4 copy-start.4
Sparse Core Ops, SparseCore 0:
  12.2 103.8 all-gather.4
  210.1 99.4 all-gather.6
where the time goes:
time: 404 us; the launch traced here: 400 us
  waiting for transfers between devices  176 us (44%)
  other arithmetic  138 us (34%)
  matrix products  35.3 us (9%)
  local copies, waits for them, and re-layouts  18.2 us (5%)
  blocking collectives  14.4 us (4%)
  between operations  14.2 us (4%)
    all_gather x2, waiting for transfers between devices, entering(): everything = lax.all_gather(shard, axis)  176 us
    select_n x128, other arithmetic, step(): return jnp.where(reached, new, before)  133 us
    unnamed x25, local copies, waits for them, and re-layouts  11.5 us
    psum x1, blocking collectives, shards(): squares = lax.psum(jnp.sum(mixed_rows * mixed_rows, axis=1), 'head')  8.42 us
  transfers between devices with their start and end apart: 2, of which 2 were waited for; matrix products, arithmetic and copies ran while one was open for 6% of the time, Pallas kernels for 0%

commit v1 on v0

--- a/solution.py
+++ b/solution.py
@@ -58,7 +58,9 @@
     )
     mixed_rows = mixed.reshape(tok_rows, -1)
     grad_float = grad_out.astype(jnp.float32)
-    squares = lax.psum(jnp.sum(mixed_rows * mixed_rows, axis=1), "head")
+    own = jnp.sum(mixed_rows * mixed_rows, axis=1)
+    blocks = lax.all_gather(own, "head", axis=0, tiled=False)
+    squares = blocks.sum(axis=0)
     inverse_rms = lax.rsqrt(squares / full_width + EPSILON)
     normed = mixed_rows * inverse_rms[:, None]
     crossed = lax.psum(jnp.sum(grad_float * normed, axis=1), "head")

time: 404 us -> 407 us (level)
    all_gather x0 -> x1, blocking collectives: none -> 9.38 us  [shards(): blocks = lax.all_gather(own, 'head', axis=0, tiled=False)]
    psum x1 -> x0, blocking collectives: 8.42 us -> none  [shards(): squares = lax.psum(jnp.sum(mixed_rows * mixed_rows, axis=1), 'head')]
where the time goes in v1:
time: 407 us; the launch traced here: 403 us
  waiting for transfers between devices  176 us (43%)
  other arithmetic  138 us (34%)
  matrix products  35.3 us (9%)
  local copies, waits for them, and re-layouts  18.2 us (4%)
  blocking collectives  17.5 us (4%)
  between operations  14.2 us (3%)
    all_gather x2, waiting for transfers between devices, entering(): everything = lax.all_gather(shard, axis)  176 us
    select_n x128, other arithmetic, step(): return jnp.where(reached, new, before)  133 us
    unnamed x25, local copies, waits for them, and re-layouts  11.5 us
    all_gather x1, blocking collectives, shards(): blocks = lax.all_gather(own, 'head', axis=0, tiled=False)  9.38 us
  transfers between devices with their start and end apart: 2, of which 2 were waited for; matrix products, arithmetic and copies ran while one was open for 6% of the time, Pallas kernels for 0%

profile of v1, /device:TPU:1, one launch (start us, length us, event | category | flops | bytes accessed | tf_op | source)
XLA Modules:
  0.0 403.0 jit_solution(1154528701728091022)
XLA Ops:
  7.2 2.4 copy.123
  9.6 2.4 fusion.10
  13.5 2.5 select_convert_fusion.1
  16.0 3.2 copy-done.1
  19.3 2.9 fusion.5
  22.2 94.0 %all-gather.6.cloned.1.call-done = f32[256,128,128]{2,1,0:T(8,128)} async-done(((f32[4,128,128]{2,1,0:T(8,128)}), f32[256,128,128]{2,1,0:T(8,128)}) %all-gather.6.cloned.1.call-update) | async-done | bytes 16777232 | tf_op jit(solution)/shard_map/all_gather | solution.py:13
  116.2 68.1 %while.30 = (s32[]{:T(128)}, f32[4,128,128]{2,1,0:T(8,128)S(1)}, s32[]{:T(128)}, f32[64,4,128,128]{3,2,1,0:T(8,128)}, s32[]{:T(128)}, /*index=5*/s32[]{:T(128)}) while((s32[]{:T(128)}, f32[4,128,128]{2,1,0:T(8,128)S(1)}, s32[]{:T(128)}, f32[64,4,128,128]{3,2,1,0:T(8,128)}, s32[]{:T(128)}, /*index=5*/s32[]{:T(128)}) %tuple.88), condition=%wide.region_1.2_spmd.clone, body=%wide.region_0.1_spmd.clone.sunk | while | flops 196612 | bytes 786533 | solution.py:22
  184.3 1.8 multiply_reduce_fusion
  186.1 1.9 copy.61
  188.0 9.4 %all-gather.1 = f32[4096]{0:T(1024)S(1)} all-gather(f32[1024]{0:T(1024)S(1)} %get-tuple-element.259), channel_id=3, replica_groups=mesh['seq'=64,'head'=4] {'head'}, dimensions={0}, use_global_device_ids=true | all-gather | bytes 20480 | tf_op jit(solution)/shard_map/all_gather | solution.py:62
  197.4 1.7 fusion
  199.2 8.1 %psum.7 = f32[1024]{0:T(1024)S(1)} all-reduce(f32[1024]{0:T(1024)S(1)} %fusion), channel_id=1, replica_groups=mesh['seq'=64,'head'=4] {'head'}, use_global_device_ids=true, to_apply=%region_5.6 | all-reduce | flops 1024 | bytes 8192 | tf_op jit(solution)/shard_map/psum | solution.py:66
  207.3 3.0 fusion.2
  210.3 1.5 copy.79
  213.1 4.3 %select_convert_fusion = bf16[4,1024,1024]{2,1,0:T(8,128)(2,1)S(1)} fusion(bf16[1024,4,128]{0,2,1:T(8,128)(2,1)S(1)} %bitcast.105, pred[1024,1024]{1,0:T(8,128)(4,1)} %copy-done.10, bf16[1024,512]{1,0:T(8,128)(2,1)} %param.10), kind=kOutput, calls=%fused_computation.2 | convolution fusion | flops 1082130432 | bytes 11534336 | tf_op jit(solution)/shard_map/thd,shd->hts/dot_general | solution.py:30
  217.5 2.9 fusion.32
  222.1 2.3 copy.74
  224.4 6.2 %fusion.33 = f32[4,128,1024]{2,1,0:T(8,128)} fusion(bf16[1024,4,128]{0,2,1:T(8,128)(2,1)S(1)} %bitcast.107, bf16[4,1024,1024]{2,1,0:T(8,128)(2,1)} %copy-done.1), kind=kOutput, calls=%fused_computation.49 | convolution fusion | flops 1073741824 | bytes 11534336 | tf_op jit(solution)/shard_map/hts,the->she/dot_general | solution.py:88
  230.6 82.1 %all-gather.8.cloned.1.call-done = f32[256,128,128]{2,1,0:T(8,128)} async-done(((f32[4,128,128]{2,1,0:T(8,128)}), f32[256,128,128]{2,1,0:T(8,128)}) %all-gather.8.cloned.1.call-update) | async-done | bytes 16777232 | tf_op jit(solution)/shard_map/all_gather | solution.py:13
  312.7 68.4 %while.31 = (s32[]{:T(128)}, f32[4,128,128]{2,1,0:T(8,128)S(1)}, s32[]{:T(128)}, f32[64,4,128,128]{3,2,1,0:T(8,128)}, s32[]{:T(128)}, /*index=5*/s32[]{:T(128)}, s32[]{:T(128)}, s32[]{:T(128)}) while((s32[]{:T(128)}, f32[4,128,128]{2,1,0:T(8,128)S(1)}, s32[]{:T(128)}, f32[64,4,128,128]{3,2,1,0:T(8,128)}, s32[]{:T(128)}, ...), condition=%wide.region_7.8_spmd.clone, body=%wide.region_6.7_spmd.clone.sunk | while | flops 196616 | bytes 786595 | solution.py:22
  381.1 3.2 fusion.7
  385.7 2.4 copy.76
  388.2 5.7 %fusion.3 = bf16[1024,4,128]{0,2,1:T(8,128)(2,1)} fusion(f32[4,128,1024]{2,1,0:T(8,128)S(1)} %copy-done.4, bf16[4,1024,1024]{2,1,0:T(8,128)(2,1)} %copy-done.2, bf16[1024,512]{1,0:T(8,128)(2,1)S(1)} %copy-done), kind=kOutput, calls=%fused_computation.11 | convolution fusion | flops 1074790400 | bytes 12582912 | tf_op jit(solution)/shard_map/hts,thd->shd/dot_general | solution.py:84
  393.9 2.3 copy.75
  (164 shorter events, 139.1 us)
Async XLA Ops:
  7.2 6.3 %copy-start = (bf16[1024,512]{1,0:T(8,128)(2,1)S(1)}, bf16[1024,512]{1,0:T(8,128)(2,1)}, u32[]{:S(2)}) copy-start(bf16[1024,512]{1,0:T(8,128)(2,1)} %param.8) | copy-start | bytes 3145732
  7.2 2.5 copy-start.7
  7.2 109.0 %all-gather.6.cloned.1.call-start = ((), (), s32[]{:S(2)}) async-start(), calls=%async_computation | async-start | bytes 17039360 | tf_op jit(solution)/shard_map/all_gather | solution.py:13
  9.6 3.8 copy-start.5
  12.1 300.6 %all-gather.8.cloned.1.call-start = ((), (), s32[]{:S(2)}) async-start(), calls=%async_computation.1 | async-start | bytes 17039360 | tf_op jit(solution)/shard_map/all_gather | solution.py:13
  12.5 1.0 copy-start.10
  13.5 5.8 %copy-start.8 = (bf16[1024,512]{1,0:T(8,128)(2,1)S(1)}, bf16[1024,512]{1,0:T(8,128)(2,1)}, u32[]{:S(2)}) copy-start(bf16[1024,512]{1,0:T(8,128)(2,1)} %param.10) | copy-start | bytes 3145732
  16.0 3.2 copy-start.1
  213.1 4.4 %copy-start.9 = (bf16[1024,512]{0,1:T(8,128)(2,1)S(1)}, bf16[1024,512]{0,1:T(8,128)(2,1)}, u32[]{:S(2)}) copy-start(bf16[1024,512]{0,1:T(8,128)(2,1)} %copy.123) | copy-start | bytes 3145732
  217.5 3.2 copy-start.2
  381.1 3.2 copy-start.3
  381.1 3.2 copy-start.6
  385.7 2.4 copy-start.4
Sparse Core Ops, SparseCore 0:
  12.2 103.8 all-gather.5
  213.2 99.4 all-gather.7
